TPU v7x, 512 devices: a whole 4x4x16 slice. The times are simulated.
512 devices in a mesh: ctx: 64 (over x, z_lo, core), head: 8 (over y, z_hi).
Axes of the slice: x: 4, y: 4, z: 16 (z_hi: 2, z_lo: 8; z = z_hi * 8 + z_lo), core: 2. Of those that a mesh axis runs over, the one named last changes fastest.
Arguments:
- queries: bfloat16 [32768, 2048], P('ctx', 'head'), may hold values from -64 to 64
- keys: bfloat16 [32768, 2048], P('ctx', 'head'), may hold values from -32 to 32
- values: bfloat16 [32768, 2048], P('ctx', 'head'), may hold values from -6 to 6
- dates: int32 [32768], P('ctx'), may hold values from 0 to 15, as said below
- plan: int32 [2], replicated, may hold values from 1 to 63, as said below
- out_weight: bfloat16 [2048, 2048], P('head'), may hold values from -0.1875 to 0.1875
Outputs:
- projected: bfloat16 [32768, 2048], P('ctx', 'head')
Inputs may be any that keep to these rules, and one draw needn't show every extreme that they name: `dates`: nondecreasing along the sequence; every date occurs. `plan`: the 2 entries differ; one of them is 63.
All inputs are finite; a program needn't handle non-finite values.
Results may differ from a plain program's by a relative error of at most 0.017.
Values may be sent and summed in bfloat16 or wider, within the bound.
A program may use at most 64 MiB of HBM per device.

v0:
```python
import jax
import jax.numpy as jnp
from jax import lax
from jax.sharding import PartitionSpec as P

HEAD_DIM = 128
ROUNDS = 2


masked_value = -1e30


def swapped(array, axis, stride):
    return lax.ppermute(array, axis, [(i, i ^ 1 << stride) for i in range(lax.axis_size(axis))])


def hop_once(travelling, bit_pos, bit_flag):
    arrived = swapped((travelling[0], travelling[1], travelling[2]), "ctx", bit_pos)
    return tuple(
        (
            jnp.where(bit_flag == 1, new_part, old_part)
            for new_part, old_part in zip(arrived, travelling)
        )
    )


def on_device(queries, keys, values, dates, plan, out_weight):
    row_count = queries.shape[0]
    heads_here = queries.shape[1] // HEAD_DIM
    score_scale = HEAD_DIM ** (-0.5)
    query_heads = queries.reshape(row_count, heads_here, HEAD_DIM)
    query_dates = dates.astype(jnp.float32)

    def attend(carry_state, key_block, value_block, key_dates):
        row_max, row_sum, accumulated = carry_state
        key_heads = key_block.reshape(-1, heads_here, HEAD_DIM)
        value_heads = value_block.reshape(-1, heads_here, HEAD_DIM)
        scores = (
            jnp.einsum("qhd,khd->hqk", query_heads, key_heads, preferred_element_type=jnp.float32)
            * score_scale
        )
        visible = key_dates[None, None, :] <= query_dates[None, :, None]
        scores = jnp.where(visible, scores, masked_value)
        new_max = jnp.maximum(row_max, jnp.max(scores, axis=-1))
        factor = jnp.exp(row_max - new_max)
        weights = jnp.where(visible, jnp.exp(scores - new_max[:, :, None]), 0.0)
        row_sum = row_sum * factor + jnp.sum(weights, axis=-1)
        product = jnp.einsum(
            "hqk,khd->qhd",
            weights.astype(jnp.bfloat16),
            value_heads,
            preferred_element_type=jnp.float32,
        )
        accumulated = accumulated * jnp.transpose(factor)[:, :, None] + product
        return (new_max, row_sum, accumulated)

    carry_state = (
        jnp.full((heads_here, row_count), masked_value, jnp.float32),
        jnp.zeros((heads_here, row_count), jnp.float32),
        jnp.zeros((row_count, heads_here, HEAD_DIM), jnp.float32),
    )
    carry_state = attend(carry_state, keys, values, query_dates)
    packed_dates = dates.astype(jnp.bfloat16)
    hop_count = lax.axis_size("ctx").bit_length() - 1
    for round_idx in range(ROUNDS):
        pattern = plan[round_idx]
        travelling = (keys, values, packed_dates)
        for bit_pos in range(hop_count):
            bit_flag = jnp.bitwise_and(jnp.right_shift(pattern, bit_pos), 1)
            travelling = hop_once(travelling, bit_pos, bit_flag)
        carry_state = attend(
            carry_state, travelling[0], travelling[1], travelling[2].astype(jnp.float32)
        )
    row_max, row_sum, accumulated = carry_state
    attended = (
        (accumulated / jnp.transpose(row_sum)[:, :, None])
        .astype(jnp.bfloat16)
        .reshape(row_count, -1)
    )
    partial_term = jnp.dot(attended, out_weight, preferred_element_type=jnp.float32)
    summed = lax.psum_scatter(
        partial_term.astype(jnp.bfloat16), "head", scatter_dimension=1, tiled=True
    )
    return summed


def solution(mesh):
    return jax.shard_map(
        on_device,
        mesh=mesh,
        in_specs=(
            P("ctx", "head"),
            P("ctx", "head"),
            P("ctx", "head"),
            P("ctx"),
            P(),
            P("head", None),
        ),
        out_specs=P("ctx", "head"),
        check_vma=False,
    )
```

profile of v0, /device:TPU:4, one launch (start us, length us, event | category | flops | bytes accessed | tf_op | source)
XLA Modules:
  0.0 409.1 jit_solution(7584251822949639296)
XLA Ops:
  24.9 3.8 collective-permute-start.18
  30.8 5.2 %collective-permute-start.19 = (bf16[512]{0:T(512)(128)(2,1)S(1)}, bf16[512]{0:T(512)(128)(2,1)S(1)}, u32[]{:S(2)}, u32[]{:S(2)}) collective-permute-start(bf16[512]{0:T(512)(128)(2,1)S(1)} %broadcast_select_fusion.23), channel_id=1, source_target_pairs={{0,32},{8,40},{16,48},{24,56},{32,0},{40,8},{48,16},{56,24},{64,96... | collective-permute-start | bytes 3080 | tf_op jit(solution)/shard_map/ppermute | solution.py:14
  36.0 3.4 collective-permute-start.2
  39.4 9.1 %collective-permute-start.20 = (bf16[512]{0:T(512)(128)(2,1)S(1)}, bf16[512]{0:T(512)(128)(2,1)S(1)}, u32[]{:S(2)}, u32[]{:S(2)}) collective-permute-start(bf16[512]{0:T(512)(128)(2,1)S(1)} %broadcast_select_fusion.24), channel_id=1, source_target_pairs={{0,64},{8,72},{16,80},{24,88},{32,96},{40,104},{48,112},{56,120},{... | collective-permute-start | bytes 3080 | tf_op jit(solution)/shard_map/ppermute | solution.py:14
  51.5 3.1 collective-permute-start.21
  54.6 3.3 collective-permute-done.3
  63.8 4.6 %collective-permute-start.5 = (bf16[512]{0:T(512)(128)(2,1)S(1)}, bf16[512]{0:T(512)(128)(2,1)S(1)}, u32[]{:S(2)}, u32[]{:S(2)}) collective-permute-start(bf16[512]{0:T(512)(128)(2,1)S(1)} %broadcast_select_fusion.31), channel_id=1, source_target_pairs={{0,256},{8,264},{16,272},{24,280},{32,288},{40,296},{48,304},{56,3... | collective-permute-start | bytes 3080 | tf_op jit(solution)/shard_map/ppermute | solution.py:14
  77.0 3.5 collective-permute-start.7
  83.9 3.5 collective-permute-start.28
  87.4 3.4 collective-permute-start.24
  90.8 7.9 %collective-permute-done.7 = bf16[512,256]{1,0:T(8,128)(2,1)S(1)} collective-permute-done((bf16[512,256]{1,0:T(8,128)(2,1)S(1)}, bf16[512,256]{1,0:T(8,128)(2,1)S(1)}, u32[]{:S(2)}, u32[]{:S(2)}) %collective-permute-start.7) | collective-permute-done | bytes 262176 | tf_op jit(solution)/shard_map/ppermute | solution.py:14
  100.7 4.5 %collective-permute-done.13 = bf16[512,256]{1,0:T(8,128)(2,1)S(1)} collective-permute-done((bf16[512,256]{1,0:T(8,128)(2,1)S(1)}, bf16[512,256]{1,0:T(8,128)(2,1)S(1)}, u32[]{:S(2)}, u32[]{:S(2)}) %collective-permute-start.13) | collective-permute-done | bytes 262176 | tf_op jit(solution)/shard_map/ppermute | solution.py:14
  108.1 4.0 collective-permute-start.29
  114.1 27.4 %collective-permute-done.8 = bf16[512,256]{1,0:T(8,128)(2,1)S(1)} collective-permute-done((bf16[512,256]{1,0:T(8,128)(2,1)S(1)}, bf16[512,256]{1,0:T(8,128)(2,1)S(1)}, u32[]{:S(2)}, u32[]{:S(2)}) %collective-permute-start.8) | collective-permute-done | bytes 262176 | tf_op jit(solution)/shard_map/ppermute | solution.py:14
  144.8 6.5 %collective-permute-start.15 = (bf16[512,256]{1,0:T(8,128)(2,1)S(1)}, bf16[512,256]{1,0:T(8,128)(2,1)S(1)}, u32[]{:S(2)}, u32[]{:S(2)}) collective-permute-start(bf16[512,256]{1,0:T(8,128)(2,1)S(1)} %broadcast_select_fusion.15), channel_id=1, source_target_pairs={{0,64},{8,72},{16,80},{24,88},{32,96},{40,104},{48,112},{56,120},{... | collective-permute-start | bytes 786440 | tf_op jit(solution)/shard_map/ppermute | solution.py:14
  151.4 10.1 %collective-permute-start.30 = (bf16[512,256]{1,0:T(8,128)(2,1)S(1)}, bf16[512,256]{1,0:T(8,128)(2,1)S(1)}, u32[]{:S(2)}, u32[]{:S(2)}) collective-permute-start(bf16[512,256]{1,0:T(8,128)(2,1)S(1)} %broadcast_select_fusion.4), channel_id=1, source_target_pairs={{0,64},{8,72},{16,80},{24,88},{32,96},{40,104},{48,112},{56,120},{... | collective-permute-start | bytes 786440 | tf_op jit(solution)/shard_map/ppermute | solution.py:14
  161.5 3.7 collective-permute-start.26
  165.3 37.0 %collective-permute-done.9 = bf16[512,256]{1,0:T(8,128)(2,1)S(1)} collective-permute-done((bf16[512,256]{1,0:T(8,128)(2,1)S(1)}, bf16[512,256]{1,0:T(8,128)(2,1)S(1)}, u32[]{:S(2)}, u32[]{:S(2)}) %collective-permute-start.9) | collective-permute-done | bytes 262176 | tf_op jit(solution)/shard_map/ppermute | solution.py:14
  204.3 3.5 collective-permute-done.15
  214.4 4.7 %collective-permute-start.27 = (bf16[512,256]{1,0:T(8,128)(2,1)}, bf16[512,256]{1,0:T(8,128)(2,1)}, u32[]{:S(2)}, u32[]{:S(2)}) collective-permute-start(bf16[512,256]{1,0:T(8,128)(2,1)} %broadcast_select_fusion.9), channel_id=1, source_target_pairs={{0,256},{8,264},{16,272},{24,280},{32,288},{40,296},{48,304},{56,3... | collective-permute-start | bytes 786440 | tf_op jit(solution)/shard_map/ppermute | solution.py:14
  219.2 4.4 %collective-permute-start.17 = (bf16[512,256]{1,0:T(8,128)(2,1)S(1)}, bf16[512,256]{1,0:T(8,128)(2,1)S(1)}, u32[]{:S(2)}, u32[]{:S(2)}) collective-permute-start(bf16[512,256]{1,0:T(8,128)(2,1)S(1)} %broadcast_select_fusion.19), channel_id=1, source_target_pairs={{0,256},{8,264},{16,272},{24,280},{32,288},{40,296},{48,304},{56,3... | collective-permute-start | bytes 786440 | tf_op jit(solution)/shard_map/ppermute | solution.py:14
  224.4 5.6 %collective-permute-start.32 = (bf16[512,256]{1,0:T(8,128)(2,1)}, bf16[512,256]{1,0:T(8,128)(2,1)}, u32[]{:S(2)}, u32[]{:S(2)}) collective-permute-start(bf16[512,256]{1,0:T(8,128)(2,1)} %broadcast_select_fusion.8), channel_id=1, source_target_pairs={{0,256},{8,264},{16,272},{24,280},{32,288},{40,296},{48,304},{56,3... | collective-permute-start | bytes 786440 | tf_op jit(solution)/shard_map/ppermute | solution.py:14
  232.6 4.4 %collective-permute-done.17 = bf16[512,256]{1,0:T(8,128)(2,1)S(1)} collective-permute-done((bf16[512,256]{1,0:T(8,128)(2,1)S(1)}, bf16[512,256]{1,0:T(8,128)(2,1)S(1)}, u32[]{:S(2)}, u32[]{:S(2)}) %collective-permute-start.17) | collective-permute-done | bytes 262176 | tf_op jit(solution)/shard_map/ppermute | solution.py:14
  255.1 147.1 %reduce-scatter.2.cloned.1.call-done = bf16[512,256]{1,0:T(8,128)(2,1)} async-done(((bf16[512,2048]{1,0:T(8,128)(2,1)}), bf16[512,256]{1,0:T(8,128)(2,1)}) %reduce-scatter.2.cloned.1.call-update) | async-done | bytes 262160 | tf_op jit(solution)/shard_map/reduce_scatter | solution.py:81
  (111 shorter events, 73.3 us)
Async XLA Ops:
  6.5 395.7 %reduce-scatter.2.cloned.1.call-start = ((), (), s32[]{:S(2)}) async-start(), calls=%async_computation.1 | async-start | bytes 2359296 | tf_op jit(solution)/shard_map/reduce_scatter | solution.py:81
  7.3 17.5 %collective-permute-start = (bf16[512]{0:T(512)(128)(2,1)S(1)}, bf16[512]{0:T(512)(128)(2,1)S(1)}, u32[]{:S(2)}, u32[]{:S(2)}) collective-permute-start(bf16[512]{0:T(512)(128)(2,1)S(1)} %get-tuple-element.21), channel_id=1, source_target_pairs={{0,8},{8,0},{16,24},{24,16},{32,40},{40,32},{48,56},{56,48},{64,72... | collective-permute-start | bytes 3080 | tf_op jit(solution)/shard_map/ppermute | solution.py:14
  9.2 62.7 %collective-permute-start.6 = (bf16[512,256]{1,0:T(8,128)(2,1)}, bf16[512,256]{1,0:T(8,128)(2,1)S(1)}, u32[]{:S(2)}, u32[]{:S(2)}) collective-permute-start(bf16[512,256]{1,0:T(8,128)(2,1)} %param.7), channel_id=1, source_target_pairs={{0,8},{8,0},{16,24},{24,16},{32,40},{40,32},{48,56},{56,48},{64,72... | collective-permute-start | bytes 786440 | tf_op jit(solution)/shard_map/ppermute | solution.py:14
  11.7 68.8 %collective-permute-start.12 = (bf16[512,256]{1,0:T(8,128)(2,1)}, bf16[512,256]{1,0:T(8,128)(2,1)}, u32[]{:S(2)}, u32[]{:S(2)}) collective-permute-start(bf16[512,256]{1,0:T(8,128)(2,1)} %param.8), channel_id=1, source_target_pairs={{0,8},{8,0},{16,24},{24,16},{32,40},{40,32},{48,56},{56,48},{64,72... | collective-permute-start | bytes 786440 | tf_op jit(solution)/shard_map/ppermute | solution.py:14
  36.0 12.5 %collective-permute-start.2 = (bf16[512]{0:T(512)(128)(2,1)S(1)}, bf16[512]{0:T(512)(128)(2,1)S(1)}, u32[]{:S(2)}, u32[]{:S(2)}) collective-permute-start(bf16[512]{0:T(512)(128)(2,1)S(1)} %broadcast_select_fusion.28), channel_id=1, source_target_pairs={{0,32},{8,40},{16,48},{24,56},{32,0},{40,8},{48,16},{56,24},{64,96... | collective-permute-start | bytes 3080 | tf_op jit(solution)/shard_map/ppermute | solution.py:14
  73.1 14.3 %collective-permute-start.23 = (bf16[512,256]{1,0:T(8,128)(2,1)S(1)}, bf16[512,256]{1,0:T(8,128)(2,1)S(1)}, u32[]{:S(2)}, u32[]{:S(2)}) collective-permute-start(bf16[512,256]{1,0:T(8,128)(2,1)S(1)} %get-tuple-element.11), channel_id=1, source_target_pairs={{0,16},{8,24},{16,0},{24,8},{32,48},{40,56},{48,32},{56,40},{64,80... | collective-permute-start | bytes 786440 | tf_op jit(solution)/shard_map/ppermute | solution.py:14
  77.0 21.7 %collective-permute-start.7 = (bf16[512,256]{1,0:T(8,128)(2,1)S(1)}, bf16[512,256]{1,0:T(8,128)(2,1)S(1)}, u32[]{:S(2)}, u32[]{:S(2)}) collective-permute-start(bf16[512,256]{1,0:T(8,128)(2,1)S(1)} %get-tuple-element.12), channel_id=1, source_target_pairs={{0,16},{8,24},{16,0},{24,8},{32,48},{40,56},{48,32},{56,40},{64,80... | collective-permute-start | bytes 786440 | tf_op jit(solution)/shard_map/ppermute | solution.py:14
  81.5 23.7 %collective-permute-start.13 = (bf16[512,256]{1,0:T(8,128)(2,1)S(1)}, bf16[512,256]{1,0:T(8,128)(2,1)S(1)}, u32[]{:S(2)}, u32[]{:S(2)}) collective-permute-start(bf16[512,256]{1,0:T(8,128)(2,1)S(1)} %get-tuple-element.10), channel_id=1, source_target_pairs={{0,16},{8,24},{16,0},{24,8},{32,48},{40,56},{48,32},{56,40},{64,80... | collective-permute-start | bytes 786440 | tf_op jit(solution)/shard_map/ppermute | solution.py:14
  83.9 24.2 %collective-permute-start.28 = (bf16[512,256]{1,0:T(8,128)(2,1)S(1)}, bf16[512,256]{1,0:T(8,128)(2,1)S(1)}, u32[]{:S(2)}, u32[]{:S(2)}) collective-permute-start(bf16[512,256]{1,0:T(8,128)(2,1)S(1)} %get-tuple-element.9), channel_id=1, source_target_pairs={{0,16},{8,24},{16,0},{24,8},{32,48},{40,56},{48,32},{56,40},{64,80... | collective-permute-start | bytes 786440 | tf_op jit(solution)/shard_map/ppermute | solution.py:14
  87.4 24.7 %collective-permute-start.24 = (bf16[512,256]{1,0:T(8,128)(2,1)S(1)}, bf16[512,256]{1,0:T(8,128)(2,1)S(1)}, u32[]{:S(2)}, u32[]{:S(2)}) collective-permute-start(bf16[512,256]{1,0:T(8,128)(2,1)S(1)} %broadcast_select_fusion.3), channel_id=1, source_target_pairs={{0,32},{8,40},{16,48},{24,56},{32,0},{40,8},{48,16},{56,24},{64,96... | collective-permute-start | bytes 786440 | tf_op jit(solution)/shard_map/ppermute | solution.py:14
  98.8 42.7 %collective-permute-start.8 = (bf16[512,256]{1,0:T(8,128)(2,1)S(1)}, bf16[512,256]{1,0:T(8,128)(2,1)S(1)}, u32[]{:S(2)}, u32[]{:S(2)}) collective-permute-start(bf16[512,256]{1,0:T(8,128)(2,1)S(1)} %broadcast_select_fusion.14), channel_id=1, source_target_pairs={{0,32},{8,40},{16,48},{24,56},{32,0},{40,8},{48,16},{56,24},{64,96... | collective-permute-start | bytes 786440 | tf_op jit(solution)/shard_map/ppermute | solution.py:14
  105.3 39.5 %collective-permute-start.14 = (bf16[512,256]{1,0:T(8,128)(2,1)S(1)}, bf16[512,256]{1,0:T(8,128)(2,1)S(1)}, u32[]{:S(2)}, u32[]{:S(2)}) collective-permute-start(bf16[512,256]{1,0:T(8,128)(2,1)S(1)} %broadcast_select_fusion.13), channel_id=1, source_target_pairs={{0,32},{8,40},{16,48},{24,56},{32,0},{40,8},{48,16},{56,24},{64,96... | collective-permute-start | bytes 786440 | tf_op jit(solution)/shard_map/ppermute | solution.py:14
  108.1 43.2 %collective-permute-start.29 = (bf16[512,256]{1,0:T(8,128)(2,1)S(1)}, bf16[512,256]{1,0:T(8,128)(2,1)S(1)}, u32[]{:S(2)}, u32[]{:S(2)}) collective-permute-start(bf16[512,256]{1,0:T(8,128)(2,1)S(1)} %broadcast_select_fusion.2), channel_id=1, source_target_pairs={{0,32},{8,40},{16,48},{24,56},{32,0},{40,8},{48,16},{56,24},{64,96... | collective-permute-start | bytes 786440 | tf_op jit(solution)/shard_map/ppermute | solution.py:14
  112.2 49.3 %collective-permute-start.25 = (bf16[512,256]{1,0:T(8,128)(2,1)S(1)}, bf16[512,256]{1,0:T(8,128)(2,1)S(1)}, u32[]{:S(2)}, u32[]{:S(2)}) collective-permute-start(bf16[512,256]{1,0:T(8,128)(2,1)S(1)} %broadcast_select_fusion.5), channel_id=1, source_target_pairs={{0,64},{8,72},{16,80},{24,88},{32,96},{40,104},{48,112},{56,120},{... | collective-permute-start | bytes 786440 | tf_op jit(solution)/shard_map/ppermute | solution.py:14
  141.5 60.8 %collective-permute-start.9 = (bf16[512,256]{1,0:T(8,128)(2,1)S(1)}, bf16[512,256]{1,0:T(8,128)(2,1)S(1)}, u32[]{:S(2)}, u32[]{:S(2)}) collective-permute-start(bf16[512,256]{1,0:T(8,128)(2,1)S(1)} %broadcast_select_fusion.16), channel_id=1, source_target_pairs={{0,64},{8,72},{16,80},{24,88},{32,96},{40,104},{48,112},{56,120},{... | collective-permute-start | bytes 786440 | tf_op jit(solution)/shard_map/ppermute | solution.py:14
  144.8 62.9 %collective-permute-start.15 = (bf16[512,256]{1,0:T(8,128)(2,1)S(1)}, bf16[512,256]{1,0:T(8,128)(2,1)S(1)}, u32[]{:S(2)}, u32[]{:S(2)}) collective-permute-start(bf16[512,256]{1,0:T(8,128)(2,1)S(1)} %broadcast_select_fusion.15), channel_id=1, source_target_pairs={{0,64},{8,72},{16,80},{24,88},{32,96},{40,104},{48,112},{56,120},{... | collective-permute-start | bytes 786440 | tf_op jit(solution)/shard_map/ppermute | solution.py:14
  151.4 59.2 %collective-permute-start.30 = (bf16[512,256]{1,0:T(8,128)(2,1)S(1)}, bf16[512,256]{1,0:T(8,128)(2,1)S(1)}, u32[]{:S(2)}, u32[]{:S(2)}) collective-permute-start(bf16[512,256]{1,0:T(8,128)(2,1)S(1)} %broadcast_select_fusion.4), channel_id=1, source_target_pairs={{0,64},{8,72},{16,80},{24,88},{32,96},{40,104},{48,112},{56,120},{... | collective-permute-start | bytes 786440 | tf_op jit(solution)/shard_map/ppermute | solution.py:14
  161.5 52.2 %collective-permute-start.26 = (bf16[512,256]{1,0:T(8,128)(2,1)S(1)}, bf16[512,256]{1,0:T(8,128)(2,1)S(1)}, u32[]{:S(2)}, u32[]{:S(2)}) collective-permute-start(bf16[512,256]{1,0:T(8,128)(2,1)S(1)} %broadcast_select_fusion.7), channel_id=1, source_target_pairs={{0,128},{8,136},{16,144},{24,152},{32,160},{40,168},{48,176},{56,1... | collective-permute-start | bytes 786440 | tf_op jit(solution)/shard_map/ppermute | solution.py:14
  202.3 27.7 %collective-permute-start.10 = (bf16[512,256]{1,0:T(8,128)(2,1)S(1)}, bf16[512,256]{1,0:T(8,128)(2,1)S(1)}, u32[]{:S(2)}, u32[]{:S(2)}) collective-permute-start(bf16[512,256]{1,0:T(8,128)(2,1)S(1)} %broadcast_select_fusion.18), channel_id=1, source_target_pairs={{0,128},{8,136},{16,144},{24,152},{32,160},{40,168},{48,176},{56,1... | collective-permute-start | bytes 786440 | tf_op jit(solution)/shard_map/ppermute | solution.py:14
  210.6 13.0 %collective-permute-start.31 = (bf16[512,256]{1,0:T(8,128)(2,1)S(1)}, bf16[512,256]{1,0:T(8,128)(2,1)S(1)}, u32[]{:S(2)}, u32[]{:S(2)}) collective-permute-start(bf16[512,256]{1,0:T(8,128)(2,1)S(1)} %broadcast_select_fusion.6), channel_id=1, source_target_pairs={{0,128},{8,136},{16,144},{24,152},{32,160},{40,168},{48,176},{56,1... | collective-permute-start | bytes 786440 | tf_op jit(solution)/shard_map/ppermute | solution.py:14
  214.4 30.8 %collective-permute-start.27 = (bf16[512,256]{1,0:T(8,128)(2,1)}, bf16[512,256]{1,0:T(8,128)(2,1)}, u32[]{:S(2)}, u32[]{:S(2)}) collective-permute-start(bf16[512,256]{1,0:T(8,128)(2,1)} %broadcast_select_fusion.9), channel_id=1, source_target_pairs={{0,256},{8,264},{16,272},{24,280},{32,288},{40,296},{48,304},{56,3... | collective-permute-start | bytes 786440 | tf_op jit(solution)/shard_map/ppermute | solution.py:14
  219.2 17.7 %collective-permute-start.17 = (bf16[512,256]{1,0:T(8,128)(2,1)S(1)}, bf16[512,256]{1,0:T(8,128)(2,1)S(1)}, u32[]{:S(2)}, u32[]{:S(2)}) collective-permute-start(bf16[512,256]{1,0:T(8,128)(2,1)S(1)} %broadcast_select_fusion.19), channel_id=1, source_target_pairs={{0,256},{8,264},{16,272},{24,280},{32,288},{40,296},{48,304},{56,3... | collective-permute-start | bytes 786440 | tf_op jit(solution)/shard_map/ppermute | solution.py:14
  224.4 17.4 %collective-permute-start.32 = (bf16[512,256]{1,0:T(8,128)(2,1)}, bf16[512,256]{1,0:T(8,128)(2,1)}, u32[]{:S(2)}, u32[]{:S(2)}) collective-permute-start(bf16[512,256]{1,0:T(8,128)(2,1)} %broadcast_select_fusion.8), channel_id=1, source_target_pairs={{0,256},{8,264},{16,272},{24,280},{32,288},{40,296},{48,304},{56,3... | collective-permute-start | bytes 786440 | tf_op jit(solution)/shard_map/ppermute | solution.py:14
  230.7 16.2 %collective-permute-start.11 = (bf16[512,256]{1,0:T(8,128)(2,1)}, bf16[512,256]{1,0:T(8,128)(2,1)}, u32[]{:S(2)}, u32[]{:S(2)}) collective-permute-start(bf16[512,256]{1,0:T(8,128)(2,1)} %broadcast_select_fusion.20), channel_id=1, source_target_pairs={{0,256},{8,264},{16,272},{24,280},{32,288},{40,296},{48,304},{56,3... | collective-permute-start | bytes 786440 | tf_op jit(solution)/shard_map/ppermute | solution.py:14
  (19 other events, 357.6 us)
Sparse Core Ops, SparseCore 0:
  255.3 146.8 reduce-scatter.1
where the time goes:
time: 411 us; the launch traced here: 409 us
  waiting for transfers between devices  243 us (59%)
  starting transfers between devices  117 us (28%)
  between operations  22.2 us (5%)
  other arithmetic  10.8 us (3%)
  matrix products  9.37 us (2%)
  local copies, waits for them, and re-layouts  7.05 us (2%)
    reduce_scatter x1, waiting for transfers between devices, on_device(): lax.psum_scatter(partial_term.astype(jnp.bfloat16), 'head', scatter_dimen...  147 us
    ppermute x33, starting transfers between devices, swapped(): lax.ppermute(array, axis, [(i, i ^ 1 << stride) for i in range(lax.axis_s...  117 us
    ppermute x33, waiting for transfers between devices, swapped(): lax.ppermute(array, axis, [(i, i ^ 1 << stride) for i in range(lax.axis_s...  95.6 us
  transfers between devices with their start and end apart: 34, of which 13 were waited for; matrix products, arithmetic and copies ran while one was open for 4% of the time, Pallas kernels for 0%

commit v1 on v0

v1 whole, which is shorter than its diff:
```python
import functools

import jax
import jax.numpy as jnp
from jax import lax
from jax.experimental import pallas as pl
from jax.experimental.pallas import tpu as pltpu
from jax.sharding import PartitionSpec as P

MESH = pl.DeviceIdType.MESH
ROWS = 512
HD = 128
NCH = 8
CROWS = ROWS // 2
WINDOW = 2
CHUNK = 128
STEPS = ROWS // CHUNK
X_PEERS = (16, 32, 48)
Z_PEERS = (2, 4, 6)
SHARE = (1, 16, 17, 32, 33, 48, 49)
EXP_SCALE = HD ** -0.5 * 1.4426950408889634
HIDDEN = -float(2 ** 30)
LOWEST = -3e38


def kernel(zstep, plan_ref, q_ref, k_ref, v_ref, d_ref, w_ref, o_ref,
           qx, kx, vx, marks, kv, kvp, farp, st1, xr, st2,
           dk, dkp, dfarp, dst1, dxr, dst2, m_ref, acc,
           om, op, wp, own, ys, yr,
           s63, r63, sc, rc, sp, rp, sx, rx, szh, rzh, sz, rz,
           sw, rw, sl, rl, sg, rg, sy, ry, credit):
    f32, bf = jnp.float32, jnp.bfloat16
    c, h = lax.axis_index("ctx"), lax.axis_index("head")
    y, zhi = h // 2, h % 2
    zlo = (c // 2) % 8
    depth = jnp.where(zlo < 4, zlo, 7 - zlo)
    far, twin, mate = (c ^ 63, h), (c, h ^ 1), (c ^ 1, h)
    over = (c ^ 14, h ^ 1)
    peers = [far, twin] + [(c, (h + 2 * j) % 8) for j in (1, 2, 3)]
    peers += [(c ^ t, h) for t in SHARE + Z_PEERS]

    barrier = pltpu.get_barrier_semaphore()
    for peer in peers:
        pl.semaphore_signal(barrier, inc=1, device_id=peer, device_id_type=MESH)

    @pl.when(depth == 0)
    def _():
        pl.semaphore_signal(barrier, inc=1, device_id=over, device_id_type=MESH)

    dk[0, 0, 0:4, :] = d_ref[...].astype(f32).astype(bf)
    dk[0, 0, 4:16, :] = jnp.zeros((12, 128), bf)
    for n in range(NCH):
        hh, which, sub = n // 4, (n // 2) % 2, n % 2
        src = (k_ref, v_ref)[which]
        kv[0, n] = src[sub * CROWS:(sub + 1) * CROWS, hh * HD:(hh + 1) * HD]
    date_ids = lax.broadcasted_iota(jnp.int32, (HD, ROWS), 0).astype(f32)

    def row_dates(s):
        block = dk[s, 0].astype(f32)
        return jnp.concatenate([block[i:i + 1, :] for i in range(4)], axis=1)

    def key_marks(s):
        marks[s] = jnp.transpose(jnp.where(row_dates(s) > date_ids, HIDDEN, 0.0)).astype(bf)

    query_marks = jnp.transpose(jnp.where(row_dates(0) == date_ids, 1.0, 0.0)).astype(bf)
    for hh in range(2):
        qx[hh, :, 0:HD] = q_ref[:, hh * HD:(hh + 1) * HD]
        qx[hh, :, HD:] = query_marks
    key_marks(0)
    vx[:, HD:] = jnp.ones((ROWS, HD), bf)
    m_ref[...] = jnp.full(m_ref.shape, LOWEST, f32)
    acc[...] = jnp.zeros(acc.shape, f32)

    other = plan_ref[0] ^ plan_ref[1] ^ 63
    crosses = (other >> 3) & 1
    pattern = other ^ (crosses * 63)
    core_bit, x_bits = pattern & 1, (pattern >> 4) & 3

    pl.semaphore_wait(barrier, len(peers) + jnp.where(depth == 0, 1, 0))

    def remote(src, dst, ss, rs, dev):
        return pltpu.make_async_remote_copy(src_ref=src, dst_ref=dst, send_sem=ss, recv_sem=rs,
                                            device_id=dev, device_id_type=MESH)

    data = (kv, kvp, farp, st1, xr, st2)
    date = (dk, dkp, dfarp, dst1, dxr, dst2)

    def to_far(b, n, i):
        return remote(b[0].at[0, n], b[0].at[1, n], s63.at[i], r63.at[i], far)

    def own_to_mate(b, i):
        return remote(b[0].at[0], b[1], sp.at[i], rp.at[i], mate)

    def far_to_mate(b, n, i):
        return remote(b[0].at[1, n], b[2].at[n], sc.at[i], rc.at[i], mate)

    def to_x(b, n, i, j):
        return remote(b[3].at[n], b[4].at[j, n], sx.at[j, i], rx.at[j, i], (c ^ X_PEERS[j], h))

    def to_z(b, n, i):
        return remote(b[5].at[n], b[0].at[2, n], szh.at[i], rzh.at[i], (c ^ zstep, h))

    def pick(flag, one, zero):
        return jnp.where(jnp.full(one.shape, flag, jnp.int32) == 1, one, zero)

    def get(ref, *at):
        return ref[at].astype(f32)

    def stage_x(b, n, i):
        far_to_mate(b, n, i).wait_recv()
        mine = pick(crosses, get(b[0], 1, n), get(b[0], 0, n))
        mates = pick(crosses, get(b[2], n), get(b[1], n))
        b[3][n] = pick(core_bit, mates, mine).astype(bf)
        for j in range(3):
            to_x(b, n, i, j).start()

    def stage_z(b, n, i):
        for j in range(3):
            to_x(b, n, i, j).wait_recv()
        low = pick(x_bits & 1, get(b[4], 0, n), get(b[3], n))
        high = pick(x_bits & 1, get(b[4], 2, n), get(b[4], 1, n))
        picked = pick(x_bits >> 1, high, low).astype(bf)
        if zstep:
            b[5][n] = picked
            to_z(b, n, i).start()
        else:
            b[0][2, n] = picked

    share = pl.ds(pl.multiple_of(((c // 16) * 2 + c % 2) * 32, 32), 32)

    def w_over(j):
        cols = pl.ds(pl.multiple_of((2 * j + 1 - zhi) * 256, 256), 256)
        return remote(w_ref.at[share, cols], wp.at[share, pl.ds(j * 256, 256)], sw.at[j], rw.at[j], over)

    def w_along():
        return remote(wp.at[share], wp.at[share], sl, rl, (c ^ jnp.where(depth == 1, 6, 2), h))

    def w_spread(j):
        return remote(wp.at[share], wp.at[share], sg.at[j], rg.at[j], (c ^ SHARE[j], h))

    def attend(s, hh):
        for sub in range(2):
            rows = slice(sub * CROWS, (sub + 1) * CROWS)
            kx[rows, 0:HD] = kv[s, 4 * hh + sub]
            vx[rows, 0:HD] = kv[s, 4 * hh + 2 + sub]
        kx[:, HD:] = marks[s]

        def step(i, _):
            rows = pl.ds(pl.multiple_of(i * CHUNK, CHUNK), CHUNK)
            scores = lax.dot_general(qx[hh, rows, :], kx[...], (((1,), (1,)), ((), ())),
                                     preferred_element_type=f32)
            old = m_ref[hh, rows, :]
            new = jnp.maximum(old, jnp.max(scores, axis=1, keepdims=True))
            p = jnp.exp2((scores - new[:, 0:1]) * EXP_SCALE).astype(bf)
            decay = jnp.exp2((old - new) * EXP_SCALE)
            acc[hh, rows, :] = (acc[hh, rows, :] * jnp.concatenate([decay, decay], axis=1)
                                + jnp.dot(p, vx[...], preferred_element_type=f32))
            m_ref[hh, rows, :] = new
            return 0

        lax.fori_loop(0, STEPS, step, 0)

    def loop(low, high, body):
        lax.fori_loop(low, high, lambda i, _: (body(i), 0)[1], 0)

    to_far(date, 0, NCH).start()
    for n in range(WINDOW):
        to_far(data, n, n).start()
    own_to_mate(date, 1).start()
    own_to_mate(data, 0).start()

    @pl.when(depth == 0)
    def _():
        for j in range(4):
            w_over(j).start()

    loop(0, 2, lambda hh: attend(0, hh))

    own_to_mate(date, 1).wait_recv()
    own_to_mate(data, 0).wait_recv()
    to_far(date, 0, NCH).wait_recv()
    far_to_mate(date, 0, NCH).start()
    key_marks(1)
    stage_x(date, 0, NCH)

    def pump(n):
        to_far(data, n, n).wait_recv()
        far_to_mate(data, n, n).start()

        @pl.when(n + WINDOW < NCH)
        def _():
            @pl.when(depth == 3)
            def _():
                for t in Z_PEERS:
                    pl.semaphore_signal(credit, inc=1, device_id=(c ^ t, h), device_id_type=MESH)

            @pl.when(depth < 3)
            def _():
                pl.semaphore_wait(credit, 1)

            to_far(data, n + WINDOW, n + WINDOW).start()

        @pl.when(n == depth)
        def _():
            @pl.when(depth == 0)
            def _():
                for j in range(4):
                    w_over(j).wait_recv()

            @pl.when(depth > 0)
            def _():
                w_along().wait_recv()

            @pl.when(depth < 3)
            def _():
                w_along().start()

            for j in range(len(SHARE)):
                w_spread(j).start()

        stage_x(data, n, n)

        @pl.when(n > 0)
        def _():
            stage_z(data, n - 1, n - 1)

    def send_o(hh, i):
        rows = pl.ds(pl.multiple_of(i * CHUNK, CHUNK), CHUNK)
        return remote(om.at[hh, rows], op.at[hh, rows], sz.at[hh, i], rz.at[hh, i], twin)

    def per_head(hh):
        loop(6 * hh, 4 + 4 * hh, pump)

        @pl.when(hh == 0)
        def _():
            stage_z(date, 0, NCH)

        @pl.when(hh == 1)
        def _():
            stage_z(data, NCH - 1, NCH - 1)
            loop(0, STEPS, lambda i: send_o(0, i).start())

        def per_block(s):
            @pl.when(s == 2)
            def _():
                loop(4 + 4 * hh, 6 + 2 * hh, pump)
                if zstep:
                    @pl.when(hh == 0)
                    def _():
                        to_z(date, 0, NCH).wait_recv()

                    loop(4 * hh, 4 * hh + 4, lambda n: to_z(data, n, n).wait_recv())

                @pl.when(hh == 0)
                def _():
                    key_marks(2)

            attend(s, hh)

        loop(1, 3, per_block)

        def close(i):
            rows = pl.ds(pl.multiple_of(i * CHUNK, CHUNK), CHUNK)
            om[hh, rows, :] = (acc[hh, rows, 0:HD] / acc[hh, rows, HD:]).astype(bf)

            @pl.when(hh == 1)
            def _():
                send_o(1, i).start()

        loop(0, STEPS, close)

    loop(0, 2, per_head)

    for j, t in enumerate(SHARE):
        peer = c ^ t
        got = wp.at[pl.ds(pl.multiple_of(((peer // 16) * 2 + peer % 2) * 32, 32), 32)]
        remote(got, got, sg.at[j], rg.at[j], (peer, h)).wait_recv()

    def to_y(j, i):
        return remote(ys.at[j - 1, i], yr.at[j - 1, i], sy.at[j - 1, i], ry.at[j - 1, i],
                      (c, (h + 2 * j) % 8))

    def project(i):
        rows = pl.ds(pl.multiple_of(i * CHUNK, CHUNK), CHUNK)
        send_o(0, i).wait_recv()
        send_o(1, i).wait_recv()

        def group(j):
            g = (y + j) % 4
            cols = pl.ds(pl.multiple_of((2 * g + zhi) * 256, 256), 256)
            pcols = pl.ds(pl.multiple_of(g * 256, 256), 256)
            mine = jnp.concatenate([om[0, rows, :], om[1, rows, :]], axis=1)
            theirs = jnp.concatenate([op[0, rows, :], op[1, rows, :]], axis=1)
            part = (jnp.dot(mine, w_ref[:, cols], preferred_element_type=f32)
                    + jnp.dot(theirs, wp[:, pcols], preferred_element_type=f32))

            @pl.when(j < 4)
            def _():
                ys[j - 1, i] = part.astype(bf)
                to_y(j, i).start()

            @pl.when(j == 4)
            def _():
                own[i] = part

        loop(1, 5, group)

    loop(0, STEPS, project)

    def finish(i):
        rows = pl.ds(pl.multiple_of(i * CHUNK, CHUNK), CHUNK)
        total = own[i]
        for j in (1, 2, 3):
            to_y(j, i).wait_recv()
            total = total + get(yr, j - 1, i)
        o_ref[rows, :] = total.astype(bf)

    loop(0, STEPS, finish)

    def left(b, n, i):
        to_far(b, n, i).wait_send()
        far_to_mate(b, n, i).wait_send()
        for j in range(3):
            to_x(b, n, i, j).wait_send()
        if zstep:
            to_z(b, n, i).wait_send()

    left(date, 0, NCH)
    loop(0, NCH, lambda n: left(data, n, n))
    own_to_mate(date, 1).wait_send()
    own_to_mate(data, 0).wait_send()

    @pl.when(depth == 0)
    def _():
        for j in range(4):
            w_over(j).wait_send()

    @pl.when(depth < 3)
    def _():
        w_along().wait_send()

    for j in range(len(SHARE)):
        w_spread(j).wait_send()

    def rest(i):
        for hh in range(2):
            send_o(hh, i).wait_send()
        for j in (1, 2, 3):
            to_y(j, i).wait_send()

    loop(0, STEPS, rest)


def call(zstep, number):
    bf, f32 = jnp.bfloat16, jnp.float32
    dma = pltpu.SemaphoreType.DMA
    vmem = pl.BlockSpec(memory_space=pltpu.VMEM)
    smem = pl.BlockSpec(memory_space=pltpu.SMEM)
    piece, dates = (CROWS, HD), (16, HD)
    return pl.pallas_call(
        functools.partial(kernel, zstep),
        out_shape=jax.ShapeDtypeStruct((ROWS, 256), bf),
        in_specs=[smem, vmem, vmem, vmem, vmem, vmem],
        out_specs=vmem,
        scratch_shapes=[
            pltpu.VMEM((2, ROWS, 256), bf),
            pltpu.VMEM((ROWS, 256), bf),
            pltpu.VMEM((ROWS, 256), bf),
            pltpu.VMEM((3, ROWS, HD), bf),
            pltpu.VMEM((3, NCH) + piece, bf),
            pltpu.VMEM((NCH,) + piece, bf),
            pltpu.VMEM((NCH,) + piece, bf),
            pltpu.VMEM((NCH,) + piece, bf),
            pltpu.VMEM((3, NCH) + piece, bf),
            pltpu.VMEM((NCH,) + piece, bf),
            pltpu.VMEM((3, 1) + dates, bf),
            pltpu.VMEM((1,) + dates, bf),
            pltpu.VMEM((1,) + dates, bf),
            pltpu.VMEM((1,) + dates, bf),
            pltpu.VMEM((3, 1) + dates, bf),
            pltpu.VMEM((1,) + dates, bf),
            pltpu.VMEM((2, ROWS, HD), f32),
            pltpu.VMEM((2, ROWS, 256), f32),
            pltpu.VMEM((2, ROWS, HD), bf),
            pltpu.VMEM((2, ROWS, HD), bf),
            pltpu.VMEM((256, 1024), bf),
            pltpu.VMEM((STEPS, CHUNK, 256), f32),
            pltpu.VMEM((3, STEPS, CHUNK, 256), bf),
            pltpu.VMEM((3, STEPS, CHUNK, 256), bf),
            dma((NCH + 1,)), dma((NCH + 1,)), dma((NCH + 1,)), dma((NCH + 1,)), dma((2,)), dma((2,)),
            dma((3, NCH + 1)), dma((3, NCH + 1)), dma((NCH + 1,)), dma((NCH + 1,)),
            dma((2, STEPS)), dma((2, STEPS)), dma((4,)), dma((4,)), dma, dma,
            dma((len(SHARE),)), dma((len(SHARE),)), dma((3, STEPS)), dma((3, STEPS)),
            pltpu.SemaphoreType.REGULAR,
        ],
        compiler_params=pltpu.CompilerParams(
            collective_id=number, has_side_effects=True, vmem_limit_bytes=48 << 20),
        cost_estimate=pl.CostEstimate(flops=1_400_000_000, bytes_accessed=3 << 20,
                                      transcendentals=1_600_000),
    )


def on_device(queries, keys, values, dates, plan, out_weight):
    other = plan[0] ^ plan[1] ^ 63
    bits = (other >> 1) & 7
    z_index = jnp.where(bits >= 4, 7 - bits, bits)
    calls = [call(2 * i, i) for i in range(4)]
    return lax.switch(z_index, calls, plan, queries, keys, values, dates.reshape(4, 128), out_weight)


def solution(mesh):
    return jax.shard_map(
        on_device,
        mesh=mesh,
        in_specs=(P("ctx", "head"), P("ctx", "head"), P("ctx", "head"), P("ctx"), P(), P("head", None)),
        out_specs=P("ctx", "head"),
        check_vma=False,
    )
```

time: 411 us -> 123 us (0.30)
  the two profiles are of different devices: /device:TPU:4 before, /device:TPU:32 now
where the time goes in v1:
time: 123 us
  Pallas kernels  119 us (97%)
  local copies, waits for them, and re-layouts  2.62 us (2%)
  between operations  1.24 us (1%)
    pallas_call x1, Pallas kernels, on_device(): lax.switch(z_index, calls, plan, queries, keys, values, dates.reshape(4,...  119 us

profile of v1, /device:TPU:32, one launch (start us, length us, event | category | flops | bytes accessed | tf_op | source)
XLA Modules:
  0.0 122.9 jit_solution(1514981814958115711)
XLA Ops:
  0.0 0.0 copy-start
  0.0 0.7 copy-done
  0.7 0.6 fusion
  2.5 0.0 copy-start.1
  2.5 0.7 copy-done.1
  3.1 119.1 %conditional.1 = (bf16[512,256]{1,0:T(8,128)(2,1)S(1)}) conditional(s32[]{:T(128)} %clamp.3, (s32[2]{0:T(128)S(1)}, bf16[512,256]{1,0:T(8,128)(2,1)}, bf16[512,256]{1,0:T(8,128)(2,1)}, bf16[512,256]{1,0:T(8,128)(2,1)}, s32[4,128]{1,0:T(4,128)S(1)}, /*index=5*/bf16[256,2048]{1,0:T(8,128)(2,1)}) %tuple.31, ...), branch_computations={%region_0.1_spmd, %region_1.2_spmd, %region_2.3_spmd, %region_3.4_... | conditional | flops 1400000000 | bytes 3145736 | solution.py:408
  3.1 119.0 %branch_0_fun.1 = bf16[512,256]{1,0:T(8,128)(2,1)S(1)} custom-call(s32[2]{0:T(128)S(1)} %get-tuple-element.56.plan_ref, bf16[512,256]{1,0:T(8,128)(2,1)} %get-tuple-element.58.q_ref, bf16[512,256]{1,0:T(8,128)(2,1)} %get-tuple-element.60.k_ref, bf16[512,256]{1,0:T(8,128)(2,1)} %get-tuple-element.61.v_ref, s32[4,128]{1,0:T(4,128)S(1)} %get-tuple-element.62.d_ref, ...), custom_call_target="tpu_custom_call" | custom-call | flops 1400000000 | bytes 3145728 | tf_op jit(solution)/shard_map/cond/branch_0_fun/pallas_call | solution.py:408
  122.2 0.7 copy.16
Async XLA Ops:
  0.0 0.7 copy-start
  2.5 0.7 copy-start.1
